TPU v7x, 32 devices: a whole 2x2x4 slice. The times are simulated.
32 devices in a mesh: ctx: 8 (over y, x, core), fsdp: 4 (over z).
Axes of the slice: x: 2, y: 2, z: 4, core: 2. Of those that a mesh axis runs over, the one named last changes fastest.
Arguments:
- layer_in: bfloat16 [4, 8, 192, 768], P('fsdp', 'ctx'), may hold values from -6 to 6
- qkv_weight: bfloat16 [768, 2304], P('fsdp'), may hold values from -0.21875 to 0.21875
- query_bias: float32 [768], replicated, may hold values from -3 to 3
- value_bias: float32 [768], replicated, may hold values from -3 to 3
- out_weight: bfloat16 [768, 768], P('fsdp'), may hold values from -1.5 to 1.5
- out_bias: float32 [768], replicated, may hold values from -3 to 3
- fc_weight: bfloat16 [768, 3072], P('fsdp'), may hold values from -0.21875 to 0.21875
- fc_bias: float32 [3072], replicated, may hold values from -3 to 3
- proj_weight: bfloat16 [3072, 768], P('fsdp'), may hold values from -0.109375 to 0.109375
- proj_bias: float32 [768], replicated, may hold values from -3 to 3
- attn_norm_gain: float32 [768], replicated, may hold values from 0.5 to 1.5
- attn_norm_shift: float32 [768], replicated, may hold values from -2 to 2
- mlp_norm_gain: float32 [768], replicated, may hold values from 0.5 to 1.5
- mlp_norm_shift: float32 [768], replicated, may hold values from -2 to 2
- cotangent: bfloat16 [4, 8, 192, 768], P('fsdp', 'ctx'), may hold values from -6 to 6
- pair_table: int32 [8], replicated, may hold values from 0 to 7, each once
Outputs:
- layer_out: bfloat16 [4, 8, 192, 768], P('fsdp', 'ctx')
- grad_in: float32 [4, 8, 192, 768], P('fsdp', 'ctx')
- grad_qkv_weight: float32 [768, 2304], P(('ctx', 'fsdp'))
- grad_query_bias: float32 [768], P(('ctx', 'fsdp'))
- grad_value_bias: float32 [768], P(('ctx', 'fsdp'))
- grad_out_weight: float32 [768, 768], P(('ctx', 'fsdp'))
- grad_out_bias: float32 [768], P(('ctx', 'fsdp'))
- grad_fc_weight: float32 [768, 3072], P(('ctx', 'fsdp'))
- grad_fc_bias: float32 [3072], P(('ctx', 'fsdp'))
- grad_proj_weight: float32 [3072, 768], P(('ctx', 'fsdp'))
- grad_proj_bias: float32 [768], P(('ctx', 'fsdp'))
- grad_attn_norm_gain: float32 [768], P(('ctx', 'fsdp'))
- grad_attn_norm_shift: float32 [768], P(('ctx', 'fsdp'))
- grad_mlp_norm_gain: float32 [768], P(('ctx', 'fsdp'))
- grad_mlp_norm_shift: float32 [768], P(('ctx', 'fsdp'))
Inputs may be any that keep to these rules, and one draw needn't show every extreme that they name: pair_table is a permutation: index c of ctx holds blocks pair_table[c] and 15 - pair_table[c] of every sequence.
All inputs are finite; a program needn't handle non-finite values.
Results may differ from a plain program's by a relative error of at most 0.035.
Values may be sent and summed in bfloat16 or wider, within the bound.
A program may use at most 256 MiB of HBM per device.

v0:
```python
from functools import partial

import jax
import jax.numpy as jnp
from jax import lax
from jax.experimental import pallas as pl
from jax.experimental.pallas import tpu as pltpu
from jax.sharding import PartitionSpec as P

H = 12
HEAD_DIM = 64
BLK = 96


epsilon = 1e-05
masked_score = -1e30


def normalize(values):
    centered = values - jnp.mean(values, axis=-1, keepdims=True)
    inverse = lax.rsqrt(jnp.mean(centered * centered, axis=-1, keepdims=True) + epsilon)
    return (centered * inverse, inverse)


def norm_back(grad_out, normed, inverse, gain):
    scaled = grad_out * gain
    grad_input = inverse * (
        scaled
        - jnp.mean(scaled, axis=-1, keepdims=True)
        - normed * jnp.mean(scaled * normed, axis=-1, keepdims=True)
    )
    return (grad_input, jnp.sum(grad_out * normed, axis=0), jnp.sum(grad_out, axis=0))


def block_positions(pair_table, device, ctx_count):
    pair_index = lax.dynamic_index_in_dim(pair_table, device, 0, keepdims=False)
    column = jnp.arange(2 * BLK, dtype=jnp.int32)
    lower = pair_index * BLK + column
    upper = (2 * ctx_count - 1 - pair_index) * BLK + column - BLK
    return jnp.where(column < BLK, lower, upper)


PAIR = 2 * HEAD_DIM
CHUNK = 8 * 2 * BLK
NT = (((1,), (1,)), ((), ()))


def chunk_of(total):
    return CHUNK if total % CHUNK == 0 else total


def head_only(block, head):
    lane = lax.broadcasted_iota(jnp.int32, block.shape, 1)
    return jnp.where((lane // HEAD_DIM) == head, block, jnp.zeros_like(block))


def head_pick(first, second):
    lane = lax.broadcasted_iota(jnp.int32, first.shape, 1)
    return jnp.where(lane < HEAD_DIM, first, second)


def dot_nt(left, right):
    return lax.dot_general(left, right, NT, preferred_element_type=jnp.float32)


def dot_nn(left, right):
    return jnp.dot(left, right, preferred_element_type=jnp.float32)


def forward_kernel(qpos_ref, kpos_ref, q_ref, k_ref, v_ref, out_ref, lse_ref, max_ref, sum_ref):
    step = pl.program_id(1)
    last = pl.num_programs(1) - 1

    @pl.when(step == 0)
    def _():
        max_ref[...] = jnp.full_like(max_ref, masked_score)
        sum_ref[...] = jnp.zeros_like(sum_ref)
        out_ref[...] = jnp.zeros_like(out_ref)

    allowed = kpos_ref[...] <= qpos_ref[...]
    query, keys, values = q_ref[...], k_ref[...], v_ref[...]
    mixed, factors = [], []
    for head in range(2):
        scores = jnp.where(allowed, dot_nt(head_only(query, head), keys), masked_score)
        old_max = max_ref[head]
        new_max = jnp.maximum(old_max, jnp.max(scores, axis=-1, keepdims=True))
        expd = jnp.exp(scores - new_max)
        factor = jnp.exp(old_max - new_max)
        sum_ref[head] = sum_ref[head] * factor + jnp.sum(expd, axis=-1, keepdims=True)
        max_ref[head] = new_max
        mixed.append(dot_nn(expd.astype(jnp.bfloat16), values))
        factors.append(factor)
    rows = query.shape[0]
    scale = head_pick(*(jnp.broadcast_to(f, (rows, PAIR)) for f in factors))
    out_ref[...] = out_ref[...] * scale + head_pick(mixed[0], mixed[1])

    @pl.when(step == last)
    def _():
        total = head_pick(*(jnp.broadcast_to(sum_ref[h], (rows, PAIR)) for h in range(2)))
        out_ref[...] = out_ref[...] / total
        lse_ref[0] = jnp.concatenate(
            [max_ref[h] + jnp.log(sum_ref[h]) for h in range(2)], axis=-1
        )


def forward_attention(query_pos, key_pos, query, keys_values):
    rows, width = query.shape
    total = keys_values.shape[0]
    chunk = chunk_of(total)
    pairs = width // PAIR
    return pl.pallas_call(
        forward_kernel,
        grid=(pairs, total // chunk),
        in_specs=[
            pl.BlockSpec((rows, 1), lambda h, c: (0, 0)),
            pl.BlockSpec((1, chunk), lambda h, c: (0, c)),
            pl.BlockSpec((rows, PAIR), lambda h, c: (0, h)),
            pl.BlockSpec((chunk, PAIR), lambda h, c: (c, h)),
            pl.BlockSpec((chunk, PAIR), lambda h, c: (c, h + pairs)),
        ],
        out_specs=[
            pl.BlockSpec((rows, PAIR), lambda h, c: (0, h)),
            pl.BlockSpec((1, rows, 2), lambda h, c: (h, 0, 0)),
        ],
        out_shape=[
            jax.ShapeDtypeStruct((rows, width), jnp.float32),
            jax.ShapeDtypeStruct((pairs, rows, 2), jnp.float32),
        ],
        scratch_shapes=[
            pltpu.VMEM((2, rows, 1), jnp.float32),
            pltpu.VMEM((2, rows, 1), jnp.float32),
        ],
        compiler_params=pltpu.CompilerParams(vmem_limit_bytes=40 * 2**20),
        cost_estimate=pl.CostEstimate(
            flops=8 * rows * total * width,
            bytes_accessed=4 * total * width,
            transcendentals=rows * total * H,
        ),
        name="attention_forward",
    )(query_pos[:, None], key_pos[None, :], query, keys_values, keys_values)


def query_kernel(qpos_ref, kpos_ref, q_ref, do_ref, stat_ref, k_ref, v_ref, dq_ref):
    @pl.when(pl.program_id(1) == 0)
    def _():
        dq_ref[...] = jnp.zeros_like(dq_ref)

    allowed = kpos_ref[...] <= qpos_ref[...]
    query, d_out, keys, values = q_ref[...], do_ref[...], k_ref[...], v_ref[...]
    parts = []
    for head in range(2):
        lse = stat_ref[0, :, head : head + 1]
        delta = stat_ref[0, :, head + 2 : head + 3]
        scores = jnp.where(allowed, dot_nt(head_only(query, head), keys), masked_score)
        prob = jnp.exp(scores - lse)
        d_prob = dot_nt(head_only(d_out, head), values)
        d_score = (prob * (d_prob - delta)).astype(jnp.bfloat16)
        parts.append(dot_nn(d_score, keys))
    dq_ref[...] += head_pick(parts[0], parts[1]) * HEAD_DIM ** (-0.5)


def query_gradient(query_pos, key_pos, query, d_out, stats, keys_values):
    rows, width = query.shape
    total = keys_values.shape[0]
    chunk = chunk_of(total)
    pairs = width // PAIR
    return pl.pallas_call(
        query_kernel,
        grid=(pairs, total // chunk),
        in_specs=[
            pl.BlockSpec((rows, 1), lambda h, c: (0, 0)),
            pl.BlockSpec((1, chunk), lambda h, c: (0, c)),
            pl.BlockSpec((rows, PAIR), lambda h, c: (0, h)),
            pl.BlockSpec((rows, PAIR), lambda h, c: (0, h)),
            pl.BlockSpec((1, rows, 4), lambda h, c: (h, 0, 0)),
            pl.BlockSpec((chunk, PAIR), lambda h, c: (c, h)),
            pl.BlockSpec((chunk, PAIR), lambda h, c: (c, h + pairs)),
        ],
        out_specs=pl.BlockSpec((rows, PAIR), lambda h, c: (0, h)),
        out_shape=jax.ShapeDtypeStruct((rows, width), jnp.float32),
        compiler_params=pltpu.CompilerParams(vmem_limit_bytes=40 * 2**20),
        cost_estimate=pl.CostEstimate(
            flops=12 * rows * total * width,
            bytes_accessed=4 * total * width,
            transcendentals=rows * total * H,
        ),
        name="attention_query_gradient",
    )(query_pos[:, None], key_pos[None, :], query, d_out, stats, keys_values, keys_values)


def key_kernel(kpos_ref, qpos_ref, k_ref, v_ref, q_ref, do_ref, stat_ref, dk_ref, dv_ref):
    @pl.when(pl.program_id(1) == 0)
    def _():
        dk_ref[...] = jnp.zeros_like(dk_ref)
        dv_ref[...] = jnp.zeros_like(dv_ref)

    allowed = kpos_ref[...] <= qpos_ref[...]
    keys, values, query, d_out = k_ref[...], v_ref[...], q_ref[...], do_ref[...]
    key_parts, value_parts = [], []
    for head in range(2):
        lse = stat_ref[0, head : head + 1, :]
        delta = stat_ref[0, head + 2 : head + 3, :]
        scores = jnp.where(allowed, dot_nt(head_only(keys, head), query), masked_score)
        prob = jnp.exp(scores - lse)
        value_parts.append(dot_nn(prob.astype(jnp.bfloat16), d_out))
        d_prob = dot_nt(head_only(values, head), d_out)
        d_score = (prob * (d_prob - delta)).astype(jnp.bfloat16)
        key_parts.append(dot_nn(d_score, query))
    dk_ref[...] += head_pick(key_parts[0], key_parts[1])
    dv_ref[...] += head_pick(value_parts[0], value_parts[1])


def key_gradients(key_pos, query_pos, qkv, query_all, d_out_all, stats_all):
    rows = qkv.shape[0]
    total, width = query_all.shape
    chunk = chunk_of(total)
    pairs = width // PAIR
    grad_spec = pl.BlockSpec((rows, PAIR), lambda h, c: (0, h))
    return pl.pallas_call(
        key_kernel,
        grid=(pairs, total // chunk),
        in_specs=[
            pl.BlockSpec((rows, 1), lambda h, c: (0, 0)),
            pl.BlockSpec((1, chunk), lambda h, c: (0, c)),
            pl.BlockSpec((rows, PAIR), lambda h, c: (0, h)),
            pl.BlockSpec((rows, PAIR), lambda h, c: (0, h + pairs)),
            pl.BlockSpec((chunk, PAIR), lambda h, c: (c, h)),
            pl.BlockSpec((chunk, PAIR), lambda h, c: (c, h)),
            pl.BlockSpec((1, 4, chunk), lambda h, c: (h, 0, c)),
        ],
        out_specs=[grad_spec, grad_spec],
        out_shape=[jax.ShapeDtypeStruct((rows, width), jnp.float32)] * 2,
        compiler_params=pltpu.CompilerParams(vmem_limit_bytes=40 * 2**20),
        cost_estimate=pl.CostEstimate(
            flops=16 * rows * total * width,
            bytes_accessed=4 * total * width,
            transcendentals=rows * total * H,
        ),
        name="attention_key_gradients",
    )(key_pos[:, None], query_pos[None, :], qkv, qkv, query_all, d_out_all, stats_all)


def whole_weight(weight):
    share = weight.shape[0] // lax.axis_size("ctx")
    mine = lax.dynamic_slice_in_dim(weight, lax.axis_index("ctx") * share, share, 0)
    return lax.all_gather(mine, ("fsdp", "ctx"), axis=0, tiled=True)


def all_positions(pair_table, ctx_count):
    column = jnp.arange(2 * BLK, dtype=jnp.int32)[None, :]
    pair = pair_table[:, None]
    lower = pair * BLK + column
    upper = (2 * ctx_count - 1 - pair) * BLK + column - BLK
    return jnp.where(column < BLK, lower, upper).reshape(-1)


def scatter(term):
    return lax.psum_scatter(term, ("ctx", "fsdp"), scatter_dimension=0, tiled=True)


def per_device(
    layer_in,
    qkv_weight,
    query_bias,
    value_bias,
    out_weight,
    out_bias,
    fc_weight,
    fc_bias,
    proj_weight,
    proj_bias,
    attn_norm_gain,
    attn_norm_shift,
    mlp_norm_gain,
    mlp_norm_shift,
    cotangent,
    pair_table,
):
    ctx_count = lax.axis_size("ctx")
    shards = ctx_count * lax.axis_size("fsdp")
    _, _, rows, width = layer_in.shape
    my_pos = block_positions(pair_table, lax.axis_index("ctx"), ctx_count)
    every_pos = all_positions(pair_table, ctx_count)
    flat_in = layer_in.reshape(rows, width).astype(jnp.float32)
    full_qkv = whole_weight(qkv_weight)
    full_out = whole_weight(out_weight)
    full_fc = whole_weight(fc_weight)
    full_proj = whole_weight(proj_weight)
    normed_one, inverse_one = normalize(flat_in)
    first_in = (normed_one * attn_norm_gain + attn_norm_shift).astype(jnp.bfloat16)
    keys_values = (
        jnp.dot(first_in, full_qkv[:, width:], preferred_element_type=jnp.float32)
        + jnp.concatenate([jnp.zeros_like(value_bias), value_bias])
    ).astype(jnp.bfloat16)
    every_kv = lax.all_gather(keys_values, "ctx", axis=0, tiled=True)
    query = (
        jnp.dot(first_in, full_qkv[:, :width], preferred_element_type=jnp.float32) + query_bias
    ).astype(jnp.bfloat16) * jnp.bfloat16(HEAD_DIM ** (-0.5))
    every_query = lax.all_gather(query, "ctx", axis=0, tiled=True)
    attn_exact, lse = forward_attention(my_pos, every_pos, query, every_kv)
    attended = attn_exact.astype(jnp.bfloat16)
    middle = flat_in + jnp.dot(attended, full_out, preferred_element_type=jnp.float32) + out_bias
    normed_two, inverse_two = normalize(middle)
    second_in = (normed_two * mlp_norm_gain + mlp_norm_shift).astype(jnp.bfloat16)
    pre_act = jnp.dot(second_in, full_fc, preferred_element_type=jnp.float32) + fc_bias
    activated, gelu_back = jax.vjp(partial(jax.nn.gelu, approximate=True), pre_act)
    act_low = activated.astype(jnp.bfloat16)
    result = middle + jnp.dot(act_low, full_proj, preferred_element_type=jnp.float32) + proj_bias
    layer_out = result.astype(jnp.bfloat16).reshape(layer_in.shape)
    d_result = cotangent.reshape(rows, width)
    d_act = jnp.einsum("td,fd->tf", d_result, full_proj, preferred_element_type=jnp.float32)
    (d_pre,) = gelu_back(d_act)
    d_pre_low = d_pre.astype(jnp.bfloat16)
    d_second = jnp.einsum("tf,df->td", d_pre_low, full_fc, preferred_element_type=jnp.float32)
    d_mid_norm, grad_mlp_gain, grad_mlp_shift = norm_back(
        d_second, normed_two, inverse_two, mlp_norm_gain
    )
    d_middle = d_result.astype(jnp.float32) + d_mid_norm
    d_branch = d_middle.astype(jnp.bfloat16)
    d_attended = jnp.einsum(
        "te,de->td", d_branch, full_out, preferred_element_type=jnp.float32
    ).astype(jnp.bfloat16)
    delta = jnp.sum(
        (d_attended.astype(jnp.float32) * attn_exact).reshape(rows, width // PAIR, 2, HEAD_DIM),
        axis=-1,
    )
    stats = jnp.concatenate([lse, jnp.transpose(delta, (1, 0, 2))], axis=-1)
    every_d_out = lax.all_gather(d_attended, "ctx", axis=0, tiled=True)
    every_stat = lax.all_gather(
        jnp.transpose(stats, (0, 2, 1)).reshape(-1, rows), "ctx", axis=1, tiled=True
    ).reshape(width // PAIR, 4, ctx_count * rows)
    grad_proj = jnp.einsum("tf,td->fd", act_low, d_result, preferred_element_type=jnp.float32)
    grad_fc = jnp.einsum("td,tf->df", second_in, d_pre_low, preferred_element_type=jnp.float32)
    grad_out = jnp.einsum("td,te->de", attended, d_branch, preferred_element_type=jnp.float32)
    sum_proj = scatter(grad_proj.astype(jnp.bfloat16))
    sum_fc = scatter(grad_fc.astype(jnp.bfloat16))
    sum_out = scatter(grad_out.astype(jnp.bfloat16))
    d_query = query_gradient(my_pos, every_pos, query, d_attended, stats, every_kv)
    d_key, d_value = key_gradients(
        my_pos, every_pos, keys_values, every_query, every_d_out, every_stat
    )
    d_qkv = jnp.concatenate([d_query, d_key, d_value], axis=1).astype(jnp.bfloat16)
    grad_qkv = jnp.einsum("td,te->de", first_in, d_qkv, preferred_element_type=jnp.float32)
    d_first = jnp.einsum("te,de->td", d_qkv, full_qkv, preferred_element_type=jnp.float32)
    d_in_norm, grad_attn_gain, grad_attn_shift = norm_back(
        d_first, normed_one, inverse_one, attn_norm_gain
    )
    grad_in = (d_middle + d_in_norm).reshape(layer_in.shape)
    bias_sum = jnp.sum(d_qkv.astype(jnp.float32), axis=0)
    vectors = (
        bias_sum[:width],
        bias_sum[2 * width :],
        jnp.sum(d_middle, axis=0),
        jnp.sum(d_pre_low.astype(jnp.float32), axis=0),
        jnp.sum(d_result.astype(jnp.float32), axis=0),
        grad_attn_gain,
        grad_attn_shift,
        grad_mlp_gain,
        grad_mlp_shift,
    )
    packed = jnp.concatenate([item.reshape(shards, -1) for item in vectors], axis=1)
    spare = -packed.shape[1] % 128
    packed = jnp.pad(packed, ((0, 0), (0, spare)))
    grad_qkv_low, packed, sum_proj, sum_fc, sum_out = lax.optimization_barrier(
        (grad_qkv.astype(jnp.bfloat16), packed, sum_proj, sum_fc, sum_out)
    )
    sum_qkv = scatter(grad_qkv_low).astype(jnp.float32)
    sum_small = scatter(packed)[0]
    small, start = [], 0
    for item in vectors:
        size = item.shape[0] // shards
        small.append(sum_small[start : start + size])
        start += size
    return (
        layer_out,
        grad_in,
        sum_qkv,
        small[0],
        small[1],
        sum_out.astype(jnp.float32),
        small[2],
        sum_fc.astype(jnp.float32),
        small[3],
        sum_proj.astype(jnp.float32),
        small[4],
        small[5],
        small[6],
        small[7],
        small[8],
    )


def solution(mesh):
    return jax.shard_map(
        per_device,
        mesh=mesh,
        in_specs=(
            P("fsdp", "ctx", None, None),
            P("fsdp", None),
            P(),
            P(),
            P("fsdp", None),
            P(),
            P("fsdp", None),
            P(),
            P("fsdp", None),
            P(),
            P(),
            P(),
            P(),
            P(),
            P("fsdp", "ctx", None, None),
            P(),
        ),
        out_specs=(
            P("fsdp", "ctx", None, None),
            P("fsdp", "ctx", None, None),
            P(("ctx", "fsdp"), None),
            P(("ctx", "fsdp")),
            P(("ctx", "fsdp")),
            P(("ctx", "fsdp"), None),
            P(("ctx", "fsdp")),
            P(("ctx", "fsdp"), None),
            P(("ctx", "fsdp")),
            P(("ctx", "fsdp"), None),
            P(("ctx", "fsdp")),
            P(("ctx", "fsdp")),
            P(("ctx", "fsdp")),
            P(("ctx", "fsdp")),
            P(("ctx", "fsdp")),
        ),
        check_vma=False,
    )
```

profile of v0, /device:TPU:0, one launch (start us, length us, event | category | flops | bytes accessed | tf_op | source)
XLA Modules:
  0.0 807.4 jit_solution(8569772587325399773)
XLA Ops:
  7.2 1.6 constant_dynamic-slice_fusion.3
  9.7 1.1 convert_reduce_fusion.3
  10.8 1.2 fusion.33
  12.0 62.3 %all-gather.9.cloned.1.call-done = bf16[768,2304]{1,0:T(8,128)(2,1)} async-done(((bf16[24,2304]{1,0:T(8,128)(2,1)}), bf16[768,2304]{1,0:T(8,128)(2,1)}) %all-gather.9.cloned.1.call-update) | async-done | bytes 3538960 | tf_op jit(solution)/shard_map/all_gather | solution.py:246
  74.3 3.3 fusion.k_ref.v_ref
  77.7 1.4 constant_dynamic-slice_fusion.2
  79.9 1.6 constant_dynamic-slice_fusion
  81.6 2.5 fusion.15.q_ref
  86.3 29.2 %all-gather.11.cloned.1.call-done.k_ref.v_ref = bf16[1536,1536]{1,0:T(8,128)(2,1)} async-done(((bf16[192,1536]{1,0:T(8,128)(2,1)}), bf16[1536,1536]{1,0:T(8,128)(2,1)}) %all-gather.11.cloned.1.call-update) | async-done | bytes 4718608 | tf_op jit(solution)/shard_map/all_gather | solution.py:295
  115.5 2.3 copy-done.1
  117.9 1.0 copy-done.3
  118.8 10.6 %attention_forward.1 = (f32[192,768]{1,0:T(8,128)S(1)}, f32[6,192,2]{2,1,0:T(8,128)S(1)}) custom-call(s32[192,1]{1,0:T(8,128)S(1)} %add_select_fusion.qpos_ref.kpos_ref, s32[1,1536]{1,0:T(1,128)S(1)} %select_n.40.kpos_ref.qpos_ref, bf16[192,768]{1,0:T(8,128)(2,1)S(1)} %copy-done.3, bf16[1536,1536]{1,0:T(8,128)(2,1)S(1)} %copy-done.1, ...), custom_call_target="tpu_custom_call" | custom-call | flops 1811939328 | bytes 4718592 | tf_op jit(solution)/shard_map/attention_forward/pallas_call | solution.py:111
  129.5 43.6 %all-gather.13.cloned.1.call-done = bf16[768,768]{1,0:T(8,128)(2,1)} async-done(((bf16[24,768]{1,0:T(8,128)(2,1)}), bf16[768,768]{1,0:T(8,128)(2,1)}) %all-gather.13.cloned.1.call-update) | async-done | bytes 1179664 | tf_op jit(solution)/shard_map/all_gather | solution.py:246
  173.1 1.8 fusion.47
  175.1 63.9 %all-gather.15.cloned.1.call-done = bf16[768,3072]{1,0:T(8,128)(2,1)} async-done(((bf16[24,3072]{1,0:T(8,128)(2,1)}), bf16[768,3072]{1,0:T(8,128)(2,1)}) %all-gather.15.cloned.1.call-update) | async-done | bytes 4718608 | tf_op jit(solution)/shard_map/all_gather | solution.py:246
  239.0 4.9 convolution_add_fusion
  243.9 60.9 %all-gather.17.cloned.1.call-done = bf16[3072,768]{1,0:T(8,128)(2,1)} async-done(((bf16[96,768]{1,0:T(8,128)(2,1)}), bf16[3072,768]{1,0:T(8,128)(2,1)}) %all-gather.17.cloned.1.call-update) | async-done | bytes 4718608 | tf_op jit(solution)/shard_map/all_gather | solution.py:246
  304.8 5.8 convert_reduce_fusion
  310.6 2.4 multiply_reduce_fusion
  313.0 1.1 fusion.45
  314.4 2.6 convert_multiply_fusion
  317.0 2.6 convolution_convert_fusion.3
  319.8 5.9 convolution_convert_fusion.2
  326.0 4.9 convolution_convert_fusion.1
  331.0 1.0 copy-done.14
  332.0 1.1 copy.36
  333.1 1.2 reduce_sum.159
  334.7 9.3 %all-gather = f32[8,192,24]{1,2,0:T(8,128)S(1)} all-gather(f32[1,192,24]{1,2,0:T(8,128)S(1)} %bitcast.98), channel_id=1, replica_groups=mesh['ctx'=8,'fsdp'=4] {'ctx'}, dimensions={0}, use_global_device_ids=true | all-gather | bytes 165888 | tf_op jit(solution)/shard_map/all_gather | solution.py:329
  344.5 2.4 copy-done.2
  347.0 8.4 %attention_query_gradient.1 = f32[192,768]{1,0:T(8,128)S(1)} custom-call(s32[192,1]{1,0:T(8,128)S(1)} %add_select_fusion.qpos_ref.kpos_ref, s32[1,1536]{1,0:T(1,128)S(1)} %select_n.40.kpos_ref.qpos_ref, bf16[192,768]{1,0:T(8,128)(2,1)S(1)} %copy-done.4, bf16[192,768]{1,0:T(8,128)(2,1)S(1)} %copy-done.5, f32[6,192,4]{2,1,0:T(8,128)S(1)} %copy.38.stat_ref, ...), custom_call_target="tpu_custom_call" | custom-call | flops 2717908992 | bytes 4718592 | tf_op jit(solution)/shard_map/attention_query_gradient/pallas_call | solution.py:167
  355.7 1.4 reshape.267
  357.1 1.4 reshape.268
  358.4 8.1 all-gather.21.cloned.1.call-done.do_ref
  366.5 1.7 copy-done.7
  368.2 1.7 copy-done.8
  369.8 10.3 %attention_key_gradients.1 = (f32[192,768]{1,0:T(8,128)S(1)}, f32[192,768]{1,0:T(8,128)S(1)}) custom-call(s32[192,1]{1,0:T(8,128)S(1)} %add_select_fusion.qpos_ref.kpos_ref, s32[1,1536]{1,0:T(1,128)S(1)} %select_n.40.kpos_ref.qpos_ref, bf16[192,1536]{1,0:T(8,128)(2,1)S(1)} %copy-done.6, bf16[192,1536]{1,0:T(8,128)(2,1)S(1)} %copy-done.6, ...), custom_call_target="tpu_custom_call" | custom-call | flops 3623878656 | bytes 4718592 | tf_op jit(solution)/shard_map/attention_key_gradients/pallas_call | solution.py:219
  380.8 3.5 fusion.32
  384.7 3.0 convolution_convert_fusion
  387.8 80.0 %reduce-scatter.9.cloned.1.call-done = bf16[24,768]{1,0:T(8,128)(2,1)} async-done(((bf16[768,768]{1,0:T(8,128)(2,1)}), bf16[24,768]{1,0:T(8,128)(2,1)}) %reduce-scatter.9.cloned.1.call-update) | async-done | bytes 36880 | tf_op jit(solution)/shard_map/reduce_scatter | solution.py:258
  467.8 111.6 %reduce-scatter.5.cloned.1.call-done = bf16[96,768]{1,0:T(8,128)(2,1)} async-done(((bf16[3072,768]{1,0:T(8,128)(2,1)}), bf16[96,768]{1,0:T(8,128)(2,1)}) %reduce-scatter.5.cloned.1.call-update) | async-done | bytes 147472 | tf_op jit(solution)/shard_map/reduce_scatter | solution.py:258
  579.4 112.3 %reduce-scatter.7.cloned.1.call-done = bf16[24,3072]{1,0:T(8,128)(2,1)} async-done(((bf16[768,3072]{1,0:T(8,128)(2,1)}), bf16[24,3072]{1,0:T(8,128)(2,1)}) %reduce-scatter.7.cloned.1.call-update) | async-done | bytes 147472 | tf_op jit(solution)/shard_map/reduce_scatter | solution.py:258
  691.7 5.3 fusion.14
  697.1 2.2 fusion.31
  699.9 0.7 convert_element_type.98
  700.6 0.7 convert_element_type.99
  701.3 40.4 %all-reduce.2 = f32[32,384]{1,0:T(8,128)S(1)} all-reduce(f32[32,384]{1,0:T(8,128)S(1)} %pad.5), channel_id=6, replica_groups=mesh['ctx'=8,'fsdp'=4] {'ctx','fsdp'}, use_global_device_ids=true, to_apply=%region_21.22.clone | all-reduce | flops 12288 | bytes 98304
  742.9 56.3 %reduce-scatter.11.cloned.1.call-done = bf16[24,2304]{1,0:T(8,128)(2,1)} async-done(((bf16[768,2304]{1,0:T(8,128)(2,1)}), bf16[24,2304]{1,0:T(8,128)(2,1)}) %reduce-scatter.11.cloned.1.call-update) | async-done | bytes 110608 | tf_op jit(solution)/shard_map/reduce_scatter | solution.py:258
  799.2 1.6 convert_element_type.96
  (127 shorter events, 7.4 us)
Async XLA Ops:
  7.2 72.0 %copy-start = (bf16[192,3072]{1,0:T(8,128)(2,1)S(1)}, bf16[192,3072]{1,0:T(8,128)(2,1)}, u32[]{:S(2)}) copy-start(bf16[192,3072]{1,0:T(8,128)(2,1)} %param.22) | copy-start | bytes 3538948
  7.2 67.1 %all-gather.9.cloned.1.call-start = ((), (), s32[]{:S(2)}) async-start(), calls=%async_computation.4 | async-start | bytes 3649536 | tf_op jit(solution)/shard_map/all_gather | solution.py:246
  8.9 106.6 %all-gather.11.cloned.1.call-start = ((), (), s32[]{:S(2)}) async-start(), calls=%async_computation.5 | async-start | bytes 5308416 | tf_op jit(solution)/shard_map/all_gather | solution.py:295
  12.0 69.6 %copy-start.28 = (f32[192]{0:T(256)}, f32[192]{0:T(256)S(1)}, u32[]{:S(2)}) copy-start(f32[192]{0:T(256)S(1)} %add_rsqrt_fusion.1) | copy-start | bytes 2308
  12.0 69.6 %copy-start.13 = (bf16[1,1,192,768]{3,2,1,0:T(8,128)(2,1)S(1)}, bf16[1,1,192,768]{3,2,1,0:T(8,128)(2,1)}, u32[]{:S(2)}) copy-start(bf16[1,1,192,768]{3,2,1,0:T(8,128)(2,1)} %param.16) | copy-start | bytes 884740
  12.0 69.6 %copy-start.26 = (f32[768]{0:T(1024)S(1)}, f32[768]{0:T(1024)}, u32[]{:S(2)}) copy-start(f32[768]{0:T(1024)} %param.26) | copy-start | bytes 9220
  12.0 69.6 %copy-start.30 = (f32[768]{0:T(1024)S(1)}, f32[768]{0:T(1024)}, u32[]{:S(2)}) copy-start(f32[768]{0:T(1024)} %param.18) | copy-start | bytes 9220
  12.0 69.6 %copy-start.31 = (f32[768]{0:T(1024)S(1)}, f32[768]{0:T(1024)}, u32[]{:S(2)}) copy-start(f32[768]{0:T(1024)} %param.27) | copy-start | bytes 9220
  77.6 6.6 copy-start.34
  77.6 95.4 %all-gather.13.cloned.1.call-start = ((), (), s32[]{:S(2)}) async-start(), calls=%async_computation.6 | async-start | bytes 1216512 | tf_op jit(solution)/shard_map/all_gather | solution.py:246
  79.1 159.9 %all-gather.15.cloned.1.call-start = ((), (), s32[]{:S(2)}) async-start(), calls=%async_computation.7 | async-start | bytes 4866048 | tf_op jit(solution)/shard_map/all_gather | solution.py:246
  79.9 224.9 %all-gather.17.cloned.1.call-start = ((), (), s32[]{:S(2)}) async-start(), calls=%async_computation.8 | async-start | bytes 4866048 | tf_op jit(solution)/shard_map/all_gather | solution.py:246
  81.5 276.9 %all-gather.19.cloned.1.call-start = ((), (), s32[]{:S(2)}) async-start(), calls=%async_computation.9 | async-start | bytes 2654208 | tf_op jit(solution)/shard_map/all_gather | solution.py:299
  84.1 282.4 %all-gather.21.cloned.1.call-start = ((), (), s32[]{:S(2)}) async-start(), calls=%async_computation.10 | async-start | bytes 2654208 | tf_op jit(solution)/shard_map/all_gather | solution.py:328
  115.5 2.3 copy-start.1
  117.8 1.0 copy-start.3
  118.8 54.3 %copy-start.25 = (f32[768]{0:T(1024)S(1)}, f32[768]{0:T(1024)}, u32[]{:S(2)}) copy-start(f32[768]{0:T(1024)} %param.21) | copy-start | bytes 9220
  129.4 109.6 %copy-start.16 = (f32[768]{0:T(1024)S(1)}, f32[768]{0:T(1024)}, u32[]{:S(2)}) copy-start(f32[768]{0:T(1024)} %param.28) | copy-start | bytes 9220
  129.4 109.6 %copy-start.18 = (f32[768]{0:T(1024)S(1)}, f32[768]{0:T(1024)}, u32[]{:S(2)}) copy-start(f32[768]{0:T(1024)} %param.29) | copy-start | bytes 9220
  129.5 109.6 %copy-start.24 = (f32[3072]{0:T(1024)S(1)}, f32[3072]{0:T(1024)}, u32[]{:S(2)}) copy-start(f32[3072]{0:T(1024)} %param.23) | copy-start | bytes 36868
  174.8 151.1 %copy-start.9 = (f32[192,768]{1,0:T(8,128)}, f32[192,768]{1,0:T(8,128)S(1)}, u32[]{:S(2)}) copy-start(f32[192,768]{1,0:T(8,128)S(1)} %get-tuple-element.59) | copy-start | bytes 1769476
  304.8 5.8 copy-start.11
  310.6 2.4 copy-start.15
  310.6 2.4 copy-start.17
  313.0 1.4 copy-start.12
  317.0 150.8 %reduce-scatter.9.cloned.1.call-start = ((), (), s32[]{:S(2)}) async-start(), calls=%async_computation.13 | async-start | bytes 1216512 | tf_op jit(solution)/shard_map/reduce_scatter | solution.py:258
  319.7 259.6 %reduce-scatter.5.cloned.1.call-start = ((), (), s32[]{:S(2)}) async-start(), calls=%async_computation.11 | async-start | bytes 4866048 | tf_op jit(solution)/shard_map/reduce_scatter | solution.py:258
  325.7 366.0 %reduce-scatter.7.cloned.1.call-start = ((), (), s32[]{:S(2)}) async-start(), calls=%async_computation.12 | async-start | bytes 4866048 | tf_op jit(solution)/shard_map/reduce_scatter | solution.py:258
  330.9 1.1 copy-start.14
  330.9 468.3 %reduce-scatter.11.cloned.1.call-start = ((), (), s32[]{:S(2)}) async-start(), calls=%async_computation.14 | async-start | bytes 3649536 | tf_op jit(solution)/shard_map/reduce_scatter | solution.py:258
  332.0 12.5 %copy-start.4 = (bf16[192,768]{1,0:T(8,128)(2,1)S(1)}, bf16[192,768]{1,0:T(8,128)(2,1)}, u32[]{:S(2)}) copy-start(bf16[192,768]{1,0:T(8,128)(2,1)} %fusion.15.q_ref) | copy-start | bytes 884740
  332.0 12.5 %copy-start.5 = (bf16[192,768]{1,0:T(8,128)(2,1)S(1)}, bf16[192,768]{1,0:T(8,128)(2,1)}, u32[]{:S(2)}) copy-start(bf16[192,768]{1,0:T(8,128)(2,1)} %get-tuple-element.62.do_ref) | copy-start | bytes 884740
  344.5 2.4 copy-start.2
  347.0 19.6 %copy-start.6 = (bf16[192,1536]{1,0:T(8,128)(2,1)S(1)}, bf16[192,1536]{1,0:T(8,128)(2,1)}, u32[]{:S(2)}) copy-start(bf16[192,1536]{1,0:T(8,128)(2,1)} %fusion.k_ref.v_ref) | copy-start | bytes 1769476
  366.5 1.7 copy-start.7
  368.2 1.7 copy-start.8
  380.1 0.7 copy-start.27
  380.2 0.7 copy-start.29
  380.8 3.7 copy-start.21
  380.8 3.7 copy-start.22
  380.8 3.9 copy-start.32
  387.8 303.9 %copy-start.10 = (f32[192,768]{1,0:T(8,128)S(1)}, f32[192,768]{1,0:T(8,128)}, u32[]{:S(2)}) copy-start(f32[192,768]{1,0:T(8,128)} %copy-done.9) | copy-start | bytes 1769476
  387.8 304.0 %copy-start.33 = (f32[768]{0:T(1024)S(1)}, f32[768]{0:T(1024)}, u32[]{:S(2)}) copy-start(f32[768]{0:T(1024)} %param.25) | copy-start | bytes 9220
  691.7 7.5 copy-start.23
  691.7 8.1 %copy-start.20 = (bf16[24,3072]{1,0:T(8,128)(2,1)S(1)}, bf16[24,3072]{1,0:T(8,128)(2,1)}, u32[]{:S(2)}) copy-start(bf16[24,3072]{1,0:T(8,128)(2,1)} %reduce-scatter.7.cloned.1.call-done) | copy-start | bytes 442372
  697.0 3.6 copy-start.19
Sparse Core Ops, SparseCore 0:
  11.5 62.7 all-gather.8
  77.8 37.6 all-gather.10
  119.0 54.0 all-gather.12
  176.4 62.5 all-gather.14
  242.3 62.4 all-gather.16
  307.1 27.8 all-gather.18
  337.4 29.0 all-gather.20
  371.6 96.1 reduce-scatter.8
  473.3 106.0 reduce-scatter.4
  585.6 106.0 reduce-scatter.6
  697.1 102.0 reduce-scatter.10
where the time goes:
time: 809 us; the launch traced here: 807 us
  waiting for transfers between devices  628 us (78%)
  blocking collectives  49.7 us (6%)
  matrix products  48.5 us (6%)
  Pallas kernels  29.3 us (4%)
  local copies, waits for them, and re-layouts  23.9 us (3%)
  between operations  15.7 us (2%)
  other arithmetic  11.1 us (1%)
    reduce_scatter x4, waiting for transfers between devices, scatter(): lax.psum_scatter(term, ('ctx', 'fsdp'), scatter_dimension=0, tiled=True)  360 us
    all_gather x4, waiting for transfers between devices, whole_weight(): return lax.all_gather(mine, ('fsdp', 'ctx'), axis=0, tiled=True)  231 us
    unnamed x1, blocking collectives  40.4 us
    all_gather x1, waiting for transfers between devices, per_device(): every_kv = lax.all_gather(keys_values, 'ctx', axis=0, tiled=True)  29.2 us
  transfers between devices with their start and end apart: 11, of which 10 were waited for; matrix products, arithmetic and copies ran while one was open for 8% of the time, Pallas kernels for 4%

commit v1 on v0

--- a/solution.py
+++ b/solution.py
@@ -244,6 +244,114 @@
     share = weight.shape[0] // lax.axis_size("ctx")
     mine = lax.dynamic_slice_in_dim(weight, lax.axis_index("ctx") * share, share, 0)
     return lax.all_gather(mine, ("fsdp", "ctx"), axis=0, tiled=True)
+
+
+def gather_kernel(chips, shards, count, *refs):
+    shares, wholes = refs[:count], refs[count : 2 * count]
+    own_sem, z_send, z_recv, c_send, c_recv, k_send, k_recv = refs[2 * count :]
+    me, row = lax.axis_index("ctx"), lax.axis_index("fsdp")
+    chip, core = me // 2, me % 2
+    sibling = (chip * 2 + 1 - core, row)
+
+    def above(step):
+        return (me, lax.rem(row + step, shards))
+
+    def across(step):
+        return (lax.rem(chip + step, chips) * 2 + core, row)
+
+    barrier = pltpu.get_barrier_semaphore()
+    greeted = [above(d) for d in range(1, shards)] + [across(d) for d in range(1, chips)]
+    greeted.append(sibling)
+    for other in greeted:
+        pl.semaphore_signal(barrier, inc=1, device_id=other, device_id_type=pl.DeviceIdType.MESH)
+    pl.semaphore_wait(barrier, len(greeted))
+
+    def send(src, dst, send_sem, recv_sem, target):
+        copy = pltpu.make_async_remote_copy(
+            src_ref=src,
+            dst_ref=dst,
+            send_sem=send_sem,
+            recv_sem=recv_sem,
+            device_id=target,
+            device_id_type=pl.DeviceIdType.MESH,
+        )
+        copy.start()
+        return copy
+
+    def column(item, index):
+        return wholes[item].at[:, index]
+
+    own, along, between, inside = {}, {}, {}, {}
+    for i in range(count):
+        own[i] = pltpu.make_async_copy(shares[i], wholes[i].at[row, me], own_sem.at[i])
+        own[i].start()
+        for d in range(1, shards):
+            along[i, d] = send(
+                shares[i],
+                wholes[i].at[row, me],
+                z_send.at[i, d - 1],
+                z_recv.at[i, d - 1],
+                above(d),
+            )
+    for i in range(count):
+        own[i].wait()
+        for d in range(1, shards):
+            along[i, d].wait_recv()
+        for d in range(1, chips):
+            mine = column(i, me)
+            between[i, d] = send(mine, mine, c_send.at[i, d - 1], c_recv.at[i, d - 1], across(d))
+        inside[i, 0] = send(
+            column(i, me), column(i, me), k_send.at[i, 0], k_recv.at[i, 0], sibling
+        )
+    for i in range(count):
+        for d in range(1, chips):
+            between[i, d].wait_recv()
+            came = column(i, lax.rem(chip - d + chips, chips) * 2 + core)
+            inside[i, d] = send(came, came, k_send.at[i, d], k_recv.at[i, d], sibling)
+    for copy in inside.values():
+        copy.wait_recv()
+    for copies in (along, between, inside):
+        for copy in copies.values():
+            copy.wait_send()
+
+
+def whole_weights(weights):
+    ctx_count, shards = lax.axis_size("ctx"), lax.axis_size("fsdp")
+    chips = ctx_count // 2
+    if ctx_count != 8:
+        return [whole_weight(item) for item in weights]
+    count = len(weights)
+    mine = []
+    for item in weights:
+        share = item.shape[0] // ctx_count
+        mine.append(
+            lax.dynamic_slice_in_dim(item, lax.axis_index("ctx") * share, share, 0)
+        )
+    anywhere = pl.BlockSpec(memory_space=pl.ANY)
+    dma = pltpu.SemaphoreType.DMA
+    wholes = pl.pallas_call(
+        partial(gather_kernel, chips, shards, count),
+        in_specs=[anywhere] * count,
+        out_specs=[anywhere] * count,
+        out_shape=[
+            jax.ShapeDtypeStruct((shards, ctx_count) + item.shape, item.dtype) for item in mine
+        ],
+        scratch_shapes=[
+            dma((count,)),
+            dma((count, shards - 1)),
+            dma((count, shards - 1)),
+            dma((count, chips - 1)),
+            dma((count, chips - 1)),
+            dma((count, chips)),
+            dma((count, chips)),
+        ],
+        compiler_params=pltpu.CompilerParams(collective_id=0, has_side_effects=True),
+        name="gather_weights",
+    )(*mine)
+    return [
+        whole.reshape(item.shape[0] * shards, item.shape[1])
+        for whole, item in zip(wholes, weights)
+    ]
 
 
 def all_positions(pair_table, ctx_count):
@@ -282,10 +390,9 @@
     my_pos = block_positions(pair_table, lax.axis_index("ctx"), ctx_count)
     every_pos = all_positions(pair_table, ctx_count)
     flat_in = layer_in.reshape(rows, width).astype(jnp.float32)
-    full_qkv = whole_weight(qkv_weight)
-    full_out = whole_weight(out_weight)
-    full_fc = whole_weight(fc_weight)
-    full_proj = whole_weight(proj_weight)
+    full_qkv, full_out, full_fc, full_proj = whole_weights(
+        (qkv_weight, out_weight, fc_weight, proj_weight)
+    )
     normed_one, inverse_one = normalize(flat_in)
     first_in = (normed_one * attn_norm_gain + attn_norm_shift).astype(jnp.bfloat16)
     keys_values = (
@@ -332,9 +439,6 @@
     grad_proj = jnp.einsum("tf,td->fd", act_low, d_result, preferred_element_type=jnp.float32)
     grad_fc = jnp.einsum("td,tf->df", second_in, d_pre_low, preferred_element_type=jnp.float32)
     grad_out = jnp.einsum("td,te->de", attended, d_branch, preferred_element_type=jnp.float32)
-    sum_proj = scatter(grad_proj.astype(jnp.bfloat16))
-    sum_fc = scatter(grad_fc.astype(jnp.bfloat16))
-    sum_out = scatter(grad_out.astype(jnp.bfloat16))
     d_query = query_gradient(my_pos, every_pos, query, d_attended, stats, every_kv)
     d_key, d_value = key_gradients(
         my_pos, every_pos, keys_values, every_query, every_d_out, every_stat
@@ -358,14 +462,29 @@
         grad_mlp_gain,
         grad_mlp_shift,
     )
-    packed = jnp.concatenate([item.reshape(shards, -1) for item in vectors], axis=1)
-    spare = -packed.shape[1] % 128
-    packed = jnp.pad(packed, ((0, 0), (0, spare)))
-    grad_qkv_low, packed, sum_proj, sum_fc, sum_out = lax.optimization_barrier(
-        (grad_qkv.astype(jnp.bfloat16), packed, sum_proj, sum_fc, sum_out)
-    )
-    sum_qkv = scatter(grad_qkv_low).astype(jnp.float32)
-    sum_small = scatter(packed)[0]
+    small = jnp.concatenate([item.reshape(shards, -1) for item in vectors], axis=1)
+    lines = 8 * -(-small.shape[1] // (8 * width))
+    small = jnp.pad(small, ((0, 0), (0, lines * width - small.shape[1])))
+    matrices = (
+        [grad_qkv[:, i * width : (i + 1) * width] for i in range(3)]
+        + [grad_out]
+        + [grad_fc[:, i * width : (i + 1) * width] for i in range(grad_fc.shape[1] // width)]
+        + [grad_proj, small.reshape(shards * lines, width)]
+    )
+    packed = jnp.concatenate(
+        [item.astype(jnp.bfloat16).reshape(shards, -1, width) for item in matrices], axis=1
+    )
+    summed = scatter(packed.reshape(-1, width)).astype(jnp.float32)
+    pieces, start = [], 0
+    for item in matrices:
+        size = item.shape[0] // shards
+        pieces.append(summed[start : start + size])
+        start += size
+    sum_qkv = jnp.concatenate(pieces[:3], axis=1)
+    sum_out = pieces[3]
+    sum_fc = jnp.concatenate(pieces[4:-2], axis=1)
+    sum_proj = pieces[-2]
+    sum_small = pieces[-1].reshape(-1)
     small, start = [], 0
     for item in vectors:
         size = item.shape[0] // shards
@@ -377,11 +496,11 @@
         sum_qkv,
         small[0],
         small[1],
-        sum_out.astype(jnp.float32),
+        sum_out,
         small[2],
-        sum_fc.astype(jnp.float32),
+        sum_fc,
         small[3],
-        sum_proj.astype(jnp.float32),
+        sum_proj,
         small[4],
         small[5],
         small[6],

time: 809 us -> 437 us (0.54)
  waiting for transfers between devices: 628 us -> 201 us
  Pallas kernels: 29.3 us -> 124 us
  blocking collectives: 49.7 us -> 9.4 us
  local copies, waits for them, and re-layouts: 23.9 us -> 46.3 us
  matrix products: 48.5 us -> 31.7 us
    all_gather x4 -> x0, waiting for transfers between devices: 231 us -> none  [whole_weight(): return lax.all_gather(mine, ('fsdp', 'ctx'), axis=0, tiled=True)]
    reduce_scatter x4 -> x1, waiting for transfers between devices: 360 us -> 158 us  [scatter(): lax.psum_scatter(term, ('ctx', 'fsdp'), scatter_dimension=0, tiled=True)]
    pallas_call x0 -> x1, Pallas kernels: none -> 94.8 us  [whole_weights(): pl.pallas_call(partial(gather_kernel, chips, shards, count), in_specs=[an...]
    unnamed x1 -> x0, blocking collectives: 40.4 us -> none
    unnamed x71 -> x99, local copies, waits for them, and re-layouts: 10.9 us -> 26.9 us
    all_gather x1, waiting for transfers between devices: 29.2 us -> 41.7 us  [per_device(): every_kv = lax.all_gather(keys_values, 'ctx', axis=0, tiled=True)]
  transfers between devices with their start and end apart: 11 -> 4, of which waited for: 10 -> 3; matrix products, arithmetic and copies ran while one was open for 8% -> 8% of each run, Pallas kernels for 4% -> 4%
where the time goes in v1:
time: 437 us; the launch traced here: 436 us
  waiting for transfers between devices  201 us (46%)
  Pallas kernels  124 us (28%)
  local copies, waits for them, and re-layouts  46.3 us (11%)
  matrix products  31.7 us (7%)
  between operations  15.6 us (4%)
  blocking collectives  9.4 us (2%)
  other arithmetic  6.95 us (2%)
    reduce_scatter x1, waiting for transfers between devices, scatter(): lax.psum_scatter(term, ('ctx', 'fsdp'), scatter_dimension=0, tiled=True)  158 us
    pallas_call x1, Pallas kernels, whole_weights(): pl.pallas_call(partial(gather_kernel, chips, shards, count), in_specs=[an...  94.8 us
    all_gather x1, waiting for transfers between devices, per_device(): every_kv = lax.all_gather(keys_values, 'ctx', axis=0, tiled=True)  41.7 us
    unnamed x99, local copies, waits for them, and re-layouts  26.9 us
    pallas_call x1, Pallas kernels, forward_attention(): pl.pallas_call(forward_kernel, grid=(pairs, total // chunk), in_specs=[pl...  10.6 us
    pallas_call x1, Pallas kernels, key_gradients(): pl.pallas_call(key_kernel, grid=(pairs, total // chunk), in_specs=[pl.Blo...  10.5 us
    all_gather x1, blocking collectives, per_device(): lax.all_gather(jnp.transpose(stats, (0, 2, 1)).reshape(-1, rows), 'ctx',...  9.4 us
  transfers between devices with their start and end apart: 4, of which 3 were waited for; matrix products, arithmetic and copies ran while one was open for 8% of the time, Pallas kernels for 4%

profile of v1, /device:TPU:0, one launch (start us, length us, event | category | flops | bytes accessed | tf_op | source)
XLA Modules:
  0.0 435.8 jit_solution(624444035876398723)
XLA Ops:
  7.2 1.6 constant_dynamic-slice_fusion.3.refs_0_
  8.9 1.4 constant_dynamic-slice_fusion.2.refs_1_
  10.9 1.1 convert_reduce_fusion
  12.0 1.2 fusion.33
  13.3 1.6 constant_dynamic-slice_fusion.refs_3_
  15.5 94.8 %gather_weights.1 = (bf16[4,8,24,2304]{3,2,1,0:T(8,128)(2,1)}, bf16[4,8,24,768]{3,2,1,0:T(8,128)(2,1)}, bf16[4,8,24,3072]{3,2,1,0:T(8,128)(2,1)}, bf16[4,8,96,768]{3,2,1,0:T(8,128)(2,1)}) custom-call(bf16[24,2304]{1,0:T(8,128)(2,1)} %constant_dynamic-slice_fusion.3.refs_0_, bf16[24,768]{1,0:T(8,128)(2,1)} %constant_dynamic-slice_fusion.2.refs_1_, ...), custom_call_target="tpu_custom_call" | custom-call | tf_op jit(solution)/shard_map/gather_weights/pallas_call | solution.py:332
  110.4 3.4 fusion.k_ref.v_ref
  113.9 2.4 fusion.15.q_ref
  118.5 41.7 %all-gather.5.cloned.1.call-done.k_ref.v_ref = bf16[1536,1536]{1,0:T(8,128)(2,1)} async-done(((bf16[192,1536]{1,0:T(8,128)(2,1)}), bf16[1536,1536]{1,0:T(8,128)(2,1)}) %all-gather.5.cloned.1.call-update) | async-done | bytes 4718608 | tf_op jit(solution)/shard_map/all_gather | solution.py:402
  160.1 2.3 copy-done.2
  162.5 1.0 copy-done.4
  163.5 10.6 %attention_forward.1 = (f32[192,768]{1,0:T(8,128)S(1)}, f32[6,192,2]{2,1,0:T(8,128)S(1)}) custom-call(s32[192,1]{1,0:T(8,128)S(1)} %add_select_fusion.qpos_ref.kpos_ref, s32[1,1536]{1,0:T(1,128)S(1)} %select_n.40.kpos_ref.qpos_ref, bf16[192,768]{1,0:T(8,128)(2,1)S(1)} %copy-done.4, bf16[1536,1536]{1,0:T(8,128)(2,1)S(1)} %copy-done.2, ...), custom_call_target="tpu_custom_call" | custom-call | flops 1811939328 | bytes 4718592 | tf_op jit(solution)/shard_map/attention_forward/pallas_call | solution.py:111
  174.9 1.2 convolution_add_fusion
  177.2 3.1 fusion.53
  180.2 2.4 multiply_reduce_fusion
  182.9 1.5 convert_multiply_fusion
  184.6 2.3 copy.36
  186.9 1.2 reduce_sum.159
  188.5 9.4 %all-gather = f32[8,192,24]{1,2,0:T(8,128)S(1)} all-gather(f32[1,192,24]{1,2,0:T(8,128)S(1)} %bitcast.111), channel_id=1, replica_groups=mesh['ctx'=8,'fsdp'=4] {'ctx'}, dimensions={0}, use_global_device_ids=true | all-gather | bytes 165888 | tf_op jit(solution)/shard_map/all_gather | solution.py:436
  198.4 2.4 copy-done.3
  200.7 8.5 %attention_query_gradient.1 = f32[192,768]{1,0:T(8,128)S(1)} custom-call(s32[192,1]{1,0:T(8,128)S(1)} %add_select_fusion.qpos_ref.kpos_ref, s32[1,1536]{1,0:T(1,128)S(1)} %select_n.40.kpos_ref.qpos_ref, bf16[192,768]{1,0:T(8,128)(2,1)S(1)} %copy-done.5, bf16[192,768]{1,0:T(8,128)(2,1)S(1)} %copy-done.6, f32[6,192,4]{2,1,0:T(8,128)S(1)} %copy.38.stat_ref, ...), custom_call_target="tpu_custom_call" | custom-call | flops 2717908992 | bytes 4718592 | tf_op jit(solution)/shard_map/attention_query_gradient/pallas_call | solution.py:167
  209.6 1.6 convolution_convert_fusion.3
  211.2 2.8 convolution_convert_fusion.2
  214.1 2.5 fusion.47
  217.3 4.2 convolution_convert_fusion.1
  221.6 1.6 all-gather.9.cloned.1.call-done.do_ref
  223.2 1.7 copy-done.8
  224.9 1.7 copy-done.9
  226.5 10.5 %attention_key_gradients.1 = (f32[192,768]{1,0:T(8,128)S(1)}, f32[192,768]{1,0:T(8,128)S(1)}) custom-call(s32[192,1]{1,0:T(8,128)S(1)} %add_select_fusion.qpos_ref.kpos_ref, s32[1,1536]{1,0:T(1,128)S(1)} %select_n.40.kpos_ref.qpos_ref, bf16[192,1536]{1,0:T(8,128)(2,1)S(1)} %copy-done.7, bf16[192,1536]{1,0:T(8,128)(2,1)S(1)} %copy-done.7, ...), custom_call_target="tpu_custom_call" | custom-call | flops 3623878656 | bytes 4718592 | tf_op jit(solution)/shard_map/attention_key_gradients/pallas_call | solution.py:219
  237.2 2.1 fusion.32
  239.3 1.2 convolution_convert_fusion
  240.7 1.2 fusion.48
  242.0 1.2 constant_dynamic-update-slice_fusion.9
  243.8 2.5 constant_dynamic-update-slice_fusion.8
  246.3 1.1 constant_dynamic-update-slice_fusion.7
  247.4 1.1 constant_dynamic-update-slice_fusion.6
  248.5 1.1 constant_dynamic-update-slice_fusion.5
  249.6 1.1 constant_dynamic-update-slice_fusion.4
  250.7 1.1 constant_dynamic-update-slice_fusion.3
  251.8 1.1 constant_dynamic-update-slice_fusion.2
  252.9 4.8 %constant_dynamic-update-slice_fusion.1 = bf16[32,296,768]{2,1,0:T(8,128)(2,1)} fusion(bf16[32,296,768]{2,1,0:T(8,128)(2,1)} %constant_dynamic-update-slice_fusion.2, bf16[32,96,768]{2,1,0:T(8,128)(2,1)} %bitcast.105), kind=kLoop, calls=%fused_computation.70 | loop fusion | bytes 9437184
  257.7 0.8 constant_dynamic-update-slice_fusion
  259.2 5.3 %fusion.14 = bf16[1,1,192,768]{3,2,1,0:T(8,128)(2,1)} fusion(f32[192,768]{1,0:T(8,128)S(1)} %get-tuple-element.71, bf16[3072,768]{1,0:T(8,128)(2,1)} %bitcast.113, f32[768]{0:T(1024)S(1)} %copy-done.40, f32[192,3072]{1,0:T(8,128)} %copy-done.18), kind=kOutput, calls=%fused_computation.28 | convolution fusion | flops 911720448 | bytes 7965696 | tf_op jit(solution)/shard_map/dot_general | solution.py:415
  264.6 1.1 fusion.31
  265.6 157.9 %reduce-scatter.2.cloned.1.call-done = bf16[296,768]{1,0:T(8,128)(2,1)} async-done(((bf16[9472,768]{1,0:T(8,128)(2,1)}), bf16[296,768]{1,0:T(8,128)(2,1)}) %reduce-scatter.2.cloned.1.call-update) | async-done | bytes 454672 | tf_op jit(solution)/shard_map/reduce_scatter | solution.py:366
  423.6 0.8 slice.159
  425.6 1.6 fusion.49
  428.6 0.7 slice.169
  (141 shorter events, 10.8 us)
Async XLA Ops:
  7.2 3.1 copy-start
  7.2 152.9 %all-gather.5.cloned.1.call-start = ((), (), s32[]{:S(2)}) async-start(), calls=%async_computation.1 | async-start | bytes 5308416 | tf_op jit(solution)/shard_map/all_gather | solution.py:402
  13.2 100.6 %copy-start.32 = (f32[192]{0:T(256)}, f32[192]{0:T(256)S(1)}, u32[]{:S(2)}) copy-start(f32[192]{0:T(256)S(1)} %add_rsqrt_fusion.1) | copy-start | bytes 2308
  110.3 3.5 copy-start.16
  110.3 3.5 copy-start.30
  110.4 3.5 copy-start.37
  110.4 3.5 copy-start.38
  113.7 2.7 copy-start.41
  113.8 107.8 %all-gather.7.cloned.1.call-start = ((), (), s32[]{:S(2)}) async-start(), calls=%async_computation.2 | async-start | bytes 2654208 | tf_op jit(solution)/shard_map/all_gather | solution.py:406
  116.3 106.9 %all-gather.9.cloned.1.call-start = ((), (), s32[]{:S(2)}) async-start(), calls=%async_computation.3 | async-start | bytes 2654208 | tf_op jit(solution)/shard_map/all_gather | solution.py:435
  160.1 2.3 copy-start.2
  162.5 1.0 copy-start.4
  163.4 10.7 %copy-start.15 = (bf16[4,8,24,768]{3,2,1,0:T(8,128)(2,1)S(1)}, bf16[4,8,24,768]{3,2,1,0:T(8,128)(2,1)}, u32[]{:S(2)}) copy-start(bf16[4,8,24,768]{3,2,1,0:T(8,128)(2,1)} %get-tuple-element.25) | copy-start | bytes 3538948
  163.4 10.7 %copy-start.29 = (f32[768]{0:T(1024)S(1)}, f32[768]{0:T(1024)}, u32[]{:S(2)}) copy-start(f32[768]{0:T(1024)} %param.21) | copy-start | bytes 9220
  163.4 11.4 %copy-start.10 = (bf16[4,8,24,3072]{3,2,1,0:T(8,128)(2,1)S(1)}, bf16[4,8,24,3072]{3,2,1,0:T(8,128)(2,1)}, u32[]{:S(2)}) copy-start(bf16[4,8,24,3072]{3,2,1,0:T(8,128)(2,1)} %get-tuple-element.26) | copy-start | bytes 14155780
  174.1 0.8 copy-start.25
  174.1 0.8 copy-start.26
  174.1 0.8 copy-start.27
  174.6 2.2 slice-start
  174.9 2.0 copy-start.22
  174.9 2.2 slice-start.1
  176.1 4.1 copy-start.18
  180.2 2.4 copy-start.21
  184.4 239.2 %reduce-scatter.2.cloned.1.call-start = ((), (), s32[]{:S(2)}) async-start(), calls=%async_computation.4 | async-start | bytes 15003648 | tf_op jit(solution)/shard_map/reduce_scatter | solution.py:366
  184.6 13.8 %copy-start.5 = (bf16[192,768]{1,0:T(8,128)(2,1)S(1)}, bf16[192,768]{1,0:T(8,128)(2,1)}, u32[]{:S(2)}) copy-start(bf16[192,768]{1,0:T(8,128)(2,1)} %fusion.15.q_ref) | copy-start | bytes 884740
  184.6 13.8 %copy-start.6 = (bf16[192,768]{1,0:T(8,128)(2,1)S(1)}, bf16[192,768]{1,0:T(8,128)(2,1)}, u32[]{:S(2)}) copy-start(bf16[192,768]{1,0:T(8,128)(2,1)} %get-tuple-element.74.do_ref) | copy-start | bytes 884740
  198.4 2.4 copy-start.3
  200.7 8.6 %copy-start.28 = (bf16[3072]{0:T(1024)(128)(2,1)S(1)}, bf16[3072]{0:T(1024)(128)(2,1)}, u32[]{:S(2)}) copy-start(bf16[3072]{0:T(1024)(128)(2,1)} %get-tuple-element.76) | copy-start | bytes 18436
  200.7 8.7 %copy-start.35 = (bf16[768]{0:T(1024)(128)(2,1)S(1)}, bf16[768]{0:T(1024)(128)(2,1)}, u32[]{:S(2)}) copy-start(bf16[768]{0:T(1024)(128)(2,1)} %get-tuple-element.31) | copy-start | bytes 4612
  200.7 8.8 %copy-start.34 = (bf16[768]{0:T(1024)(128)(2,1)S(1)}, bf16[768]{0:T(1024)(128)(2,1)}, u32[]{:S(2)}) copy-start(bf16[768]{0:T(1024)(128)(2,1)} %get-tuple-element.37) | copy-start | bytes 4612
  214.0 3.1 copy-start.19
  214.0 3.3 copy-start.23
  217.3 5.9 %copy-start.7 = (bf16[192,1536]{1,0:T(8,128)(2,1)S(1)}, bf16[192,1536]{1,0:T(8,128)(2,1)}, u32[]{:S(2)}) copy-start(bf16[192,1536]{1,0:T(8,128)(2,1)} %fusion.k_ref.v_ref) | copy-start | bytes 1769476
  217.3 19.8 %copy-start.31 = (f32[768]{0:T(1024)S(1)}, f32[768]{0:T(1024)}, u32[]{:S(2)}) copy-start(f32[768]{0:T(1024)} %param.26) | copy-start | bytes 9220
  217.3 19.8 %copy-start.33 = (f32[192]{0:T(256)S(1)}, f32[192]{0:T(256)}, u32[]{:S(2)}) copy-start(f32[192]{0:T(256)} %copy-done.32) | copy-start | bytes 2308
  223.2 1.7 copy-start.8
  224.9 1.7 copy-start.9
  226.5 10.7 %copy-start.36 = (bf16[4,8,24,2304]{3,2,1,0:T(8,128)(2,1)S(1)}, bf16[4,8,24,2304]{3,2,1,0:T(8,128)(2,1)}, u32[]{:S(2)}) copy-start(bf16[4,8,24,2304]{3,2,1,0:T(8,128)(2,1)} %get-tuple-element.23) | copy-start | bytes 10616836
  237.2 2.2 copy-start.39
  243.8 3.6 copy-start.17
  246.2 2.2 copy-start.14
  247.3 2.3 copy-start.13
  248.5 2.2 copy-start.12
  249.6 2.2 copy-start.11
  258.5 0.7 copy-start.40
  259.2 5.3 %copy-start.24 = (f32[192,768]{1,0:T(8,128)S(1)}, f32[192,768]{1,0:T(8,128)}, u32[]{:S(2)}) copy-start(f32[192,768]{1,0:T(8,128)} %get-tuple-element.75) | copy-start | bytes 1769476
  264.6 164.7 %copy-start.1 = (bf16[192,3072]{1,0:T(8,128)(2,1)S(1)}, bf16[192,3072]{1,0:T(8,128)(2,1)}, u32[]{:S(2)}) copy-start(bf16[192,3072]{1,0:T(8,128)(2,1)} %param.22) | copy-start | bytes 3538948
  423.6 5.0 %copy-start.20 = (bf16[296,768]{1,0:T(8,128)(2,1)S(1)}, bf16[296,768]{1,0:T(8,128)(2,1)}, u32[]{:S(2)}) copy-start(bf16[296,768]{1,0:T(8,128)(2,1)} %reduce-scatter.2.cloned.1.call-done) | copy-start | bytes 1363972
Sparse Core Ops, SparseCore 0:
  113.9 46.2 all-gather.4
  162.6 29.0 all-gather.6
  194.1 29.0 all-gather.8
  258.7 164.8 reduce-scatter.1

commit v2 on v1

--- a/solution.py
+++ b/solution.py
@@ -354,6 +354,143 @@
     ]
 
 
+def scatter_kernel(chips, shards, spans, packed, out, own, k_land, c_land, z_land, *sems):
+    local, k_send, k_recv, c_send, c_recv, z_send, z_recv = sems
+    me, row = lax.axis_index("ctx"), lax.axis_index("fsdp")
+    chip, core = me // 2, me % 2
+    sibling = (chip * 2 + 1 - core, row)
+
+    def above(step):
+        return (me, lax.rem(row + step, shards))
+
+    def across(step):
+        return (lax.rem(chip + step, chips) * 2 + core, row)
+
+    barrier = pltpu.get_barrier_semaphore()
+    greeted = [above(d) for d in range(1, shards)] + [across(d) for d in range(1, chips)]
+    greeted.append(sibling)
+    for other in greeted:
+        pl.semaphore_signal(barrier, inc=1, device_id=other, device_id_type=pl.DeviceIdType.MESH)
+    pl.semaphore_wait(barrier, len(greeted))
+
+    def send(src, dst, send_sem, recv_sem, target):
+        copy = pltpu.make_async_remote_copy(
+            src_ref=src,
+            dst_ref=dst,
+            send_sem=send_sem,
+            recv_sem=recv_sem,
+            device_id=target,
+            device_id_type=pl.DeviceIdType.MESH,
+        )
+        copy.start()
+        return copy
+
+    order = list(range(1, chips)) + [0]
+    kept, inside, between, along = {}, {}, {}, {}
+    for i, span in enumerate(spans):
+        rows = pl.ds(*span)
+        for d in order:
+            part = lax.rem(chip + d, chips)
+            inside[i, d] = send(
+                packed.at[part, 1 - core, :, rows],
+                k_land.at[part, :, rows],
+                k_send.at[i, d],
+                k_recv.at[i, d],
+                sibling,
+            )
+            kept[i, d] = pltpu.make_async_copy(
+                packed.at[part, core, :, rows], own.at[part, :, rows], local.at[i, d]
+            )
+            kept[i, d].start()
+    for i, span in enumerate(spans):
+        rows = pl.ds(*span)
+        for d in order:
+            part = lax.rem(chip + d, chips)
+            kept[i, d].wait()
+            inside[i, d].wait_recv()
+
+            @pl.loop(0, shards)
+            def _(f):
+                total = own[part, f, rows].astype(jnp.float32)
+                total += k_land[part, f, rows].astype(jnp.float32)
+                own[part, f, rows] = total.astype(jnp.bfloat16)
+
+            if d:
+                between[i, d] = send(
+                    own.at[part, :, rows],
+                    c_land.at[d - 1, :, rows],
+                    c_send.at[i, d - 1],
+                    c_recv.at[i, d - 1],
+                    across(d),
+                )
+    for i, span in enumerate(spans):
+        rows = pl.ds(*span)
+        for d in range(1, chips):
+            between[i, d].wait_recv()
+
+        @pl.loop(0, shards)
+        def _(f):
+            total = own[chip, f, rows].astype(jnp.float32)
+            for d in range(1, chips):
+                total += c_land[d - 1, f, rows].astype(jnp.float32)
+            own[chip, f, rows] = total.astype(jnp.bfloat16)
+
+        for d in range(1, shards):
+            along[i, d] = send(
+                own.at[chip, lax.rem(row + d, shards), rows],
+                z_land.at[d - 1, rows],
+                z_send.at[i, d - 1],
+                z_recv.at[i, d - 1],
+                above(d),
+            )
+    for i, span in enumerate(spans):
+        rows = pl.ds(*span)
+        for d in range(1, shards):
+            along[i, d].wait_recv()
+        total = own[chip, row, rows].astype(jnp.float32)
+        for d in range(1, shards):
+            total += z_land[d - 1, rows].astype(jnp.float32)
+        out[rows] = total
+    for copies in (inside, between, along):
+        for copy in copies.values():
+            copy.wait_send()
+
+
+def scatter_packed(packed):
+    ctx_count, shards = lax.axis_size("ctx"), lax.axis_size("fsdp")
+    _, rows, width = packed.shape
+    if ctx_count != 8:
+        return scatter(packed.reshape(-1, width)).astype(jnp.float32)
+    chips = ctx_count // 2
+    first = 16 * (-(-rows // 32))
+    spans = ((0, first), (first, rows - first))
+    dma = pltpu.SemaphoreType.DMA
+    low = jnp.bfloat16
+    return pl.pallas_call(
+        partial(scatter_kernel, chips, shards, spans),
+        in_specs=[pl.BlockSpec(memory_space=pl.ANY)],
+        out_specs=pl.BlockSpec(memory_space=pltpu.VMEM),
+        out_shape=jax.ShapeDtypeStruct((rows, width), jnp.float32),
+        scratch_shapes=[
+            pltpu.VMEM((chips, shards, rows, width), low),
+            pltpu.VMEM((chips, shards, rows, width), low),
+            pltpu.VMEM((chips - 1, shards, rows, width), low),
+            pltpu.VMEM((shards - 1, rows, width), low),
+            dma((2, chips)),
+            dma((2, chips)),
+            dma((2, chips)),
+            dma((2, chips - 1)),
+            dma((2, chips - 1)),
+            dma((2, shards - 1)),
+            dma((2, shards - 1)),
+        ],
+        compiler_params=pltpu.CompilerParams(
+            collective_id=1, has_side_effects=True, vmem_limit_bytes=44 * 2**20
+        ),
+        name="sum_gradients",
+    )(packed.reshape(chips, 2, shards, rows, width))
+
+
 def all_positions(pair_table, ctx_count):
     column = jnp.arange(2 * BLK, dtype=jnp.int32)[None, :]
     pair = pair_table[:, None]
@@ -463,7 +600,7 @@
         grad_mlp_shift,
     )
     small = jnp.concatenate([item.reshape(shards, -1) for item in vectors], axis=1)
-    lines = 8 * -(-small.shape[1] // (8 * width))
+    lines = 16 * -(-small.shape[1] // (16 * width))
     small = jnp.pad(small, ((0, 0), (0, lines * width - small.shape[1])))
     matrices = (
         [grad_qkv[:, i * width : (i + 1) * width] for i in range(3)]
@@ -474,7 +611,7 @@
     packed = jnp.concatenate(
         [item.astype(jnp.bfloat16).reshape(shards, -1, width) for item in matrices], axis=1
     )
-    summed = scatter(packed.reshape(-1, width)).astype(jnp.float32)
+    summed = scatter_packed(packed)
     pieces, start = [], 0
     for item in matrices:
         size = item.shape[0] // shards

time: 437 us -> 386 us (0.88)
  waiting for transfers between devices: 201 us -> 41.7 us
  Pallas kernels: 124 us -> 231 us
    reduce_scatter x1 -> x0, waiting for transfers between devices: 158 us -> none  [scatter(): lax.psum_scatter(term, ('ctx', 'fsdp'), scatter_dimension=0, tiled=True)]
    pallas_call x0 -> x1, Pallas kernels: none -> 106 us  [scatter_packed(): pl.pallas_call(partial(scatter_kernel, chips, shards, spans), in_specs=[p...]
    unnamed x99 -> x125, local copies, waits for them, and re-layouts: 26.9 us -> 25 us
  transfers between devices with their start and end apart: 4 -> 3, of which waited for: 3 -> 1; matrix products, arithmetic and copies ran while one was open for 8% -> 9% of each run, Pallas kernels for 4% -> 5%
where the time goes in v2:
time: 386 us; the launch traced here: 383 us
  Pallas kernels  231 us (60%)
  local copies, waits for them, and re-layouts  47.4 us (12%)
  waiting for transfers between devices  41.7 us (11%)
  matrix products  29.2 us (8%)
  between operations  15.8 us (4%)
  blocking collectives  9.4 us (2%)
  other arithmetic  8.63 us (2%)
    pallas_call x1, Pallas kernels, scatter_packed(): pl.pallas_call(partial(scatter_kernel, chips, shards, spans), in_specs=[p...  106 us
    pallas_call x1, Pallas kernels, whole_weights(): pl.pallas_call(partial(gather_kernel, chips, shards, count), in_specs=[an...  94.8 us
    all_gather x1, waiting for transfers between devices, per_device(): every_kv = lax.all_gather(keys_values, 'ctx', axis=0, tiled=True)  41.7 us
    unnamed x125, local copies, waits for them, and re-layouts  25 us
    pallas_call x1, Pallas kernels, forward_attention(): pl.pallas_call(forward_kernel, grid=(pairs, total // chunk), in_specs=[pl...  10.6 us
    pallas_call x1, Pallas kernels, key_gradients(): pl.pallas_call(key_kernel, grid=(pairs, total // chunk), in_specs=[pl.Blo...  10.5 us
    all_gather x1, blocking collectives, per_device(): lax.all_gather(jnp.transpose(stats, (0, 2, 1)).reshape(-1, rows), 'ctx',...  9.4 us
    pallas_call x1, Pallas kernels, query_gradient(): pl.pallas_call(query_kernel, grid=(pairs, total // chunk), in_specs=[pl.B...  8.48 us
  transfers between devices with their start and end apart: 3, of which 1 were waited for; matrix products, arithmetic and copies ran while one was open for 9% of the time, Pallas kernels for 5%

profile of v2, /device:TPU:0, one launch (start us, length us, event | category | flops | bytes accessed | tf_op | source)
XLA Modules:
  0.0 382.9 jit_solution(10466890652293326938)
XLA Ops:
  7.2 1.6 constant_dynamic-slice_fusion.3.refs_0_
  8.9 1.4 constant_dynamic-slice_fusion.2.refs_1_
  10.9 1.1 convert_reduce_fusion
  12.1 1.2 fusion.33
  13.3 1.6 constant_dynamic-slice_fusion.refs_3_
  15.5 94.8 %gather_weights.1 = (bf16[4,8,24,2304]{3,2,1,0:T(8,128)(2,1)}, bf16[4,8,24,768]{3,2,1,0:T(8,128)(2,1)}, bf16[4,8,24,3072]{3,2,1,0:T(8,128)(2,1)}, bf16[4,8,96,768]{3,2,1,0:T(8,128)(2,1)}) custom-call(bf16[24,2304]{1,0:T(8,128)(2,1)} %constant_dynamic-slice_fusion.3.refs_0_, bf16[24,768]{1,0:T(8,128)(2,1)} %constant_dynamic-slice_fusion.2.refs_1_, ...), custom_call_target="tpu_custom_call" | custom-call | tf_op jit(solution)/shard_map/gather_weights/pallas_call | solution.py:332
  110.4 3.4 fusion.k_ref.v_ref
  113.9 2.4 fusion.15.q_ref
  118.5 41.7 %all-gather.5.cloned.1.call-done.k_ref.v_ref = bf16[1536,1536]{1,0:T(8,128)(2,1)} async-done(((bf16[192,1536]{1,0:T(8,128)(2,1)}), bf16[1536,1536]{1,0:T(8,128)(2,1)}) %all-gather.5.cloned.1.call-update) | async-done | bytes 4718608 | tf_op jit(solution)/shard_map/all_gather | solution.py:539
  160.2 2.3 copy-done.2
  162.5 1.0 copy-done.4
  163.5 10.6 %attention_forward.1 = (f32[192,768]{1,0:T(8,128)S(1)}, f32[6,192,2]{2,1,0:T(8,128)S(1)}) custom-call(s32[192,1]{1,0:T(8,128)S(1)} %add_select_fusion.qpos_ref.kpos_ref, s32[1,1536]{1,0:T(1,128)S(1)} %select_n.40.kpos_ref.qpos_ref, bf16[192,768]{1,0:T(8,128)(2,1)S(1)} %copy-done.4, bf16[1536,1536]{1,0:T(8,128)(2,1)S(1)} %copy-done.2, ...), custom_call_target="tpu_custom_call" | custom-call | flops 1811939328 | bytes 4718592 | tf_op jit(solution)/shard_map/attention_forward/pallas_call | solution.py:111
  175.0 1.2 convolution_add_fusion
  177.2 3.1 fusion.53
  180.2 2.4 multiply_reduce_fusion
  182.6 0.9 fusion.46
  183.5 1.5 convert_multiply_fusion
  185.2 2.3 copy.36
  187.5 1.3 reduce_sum.159
  189.0 9.4 %all-gather = f32[8,192,24]{1,2,0:T(8,128)S(1)} all-gather(f32[1,192,24]{1,2,0:T(8,128)S(1)} %bitcast.110), channel_id=1, replica_groups=mesh['ctx'=8,'fsdp'=4] {'ctx'}, dimensions={0}, use_global_device_ids=true | all-gather | bytes 165888 | tf_op jit(solution)/shard_map/all_gather | solution.py:573
  199.0 2.4 copy-done.3
  201.4 8.5 %attention_query_gradient.1 = f32[192,768]{1,0:T(8,128)S(1)} custom-call(s32[192,1]{1,0:T(8,128)S(1)} %add_select_fusion.qpos_ref.kpos_ref, s32[1,1536]{1,0:T(1,128)S(1)} %select_n.40.kpos_ref.qpos_ref, bf16[192,768]{1,0:T(8,128)(2,1)S(1)} %copy-done.5, bf16[192,768]{1,0:T(8,128)(2,1)S(1)} %copy-done.6, f32[6,192,4]{2,1,0:T(8,128)S(1)} %copy.38.stat_ref, ...), custom_call_target="tpu_custom_call" | custom-call | flops 2717908992 | bytes 4718592 | tf_op jit(solution)/shard_map/attention_query_gradient/pallas_call | solution.py:167
  212.1 1.6 convolution_convert_fusion.3
  213.7 2.8 convolution_convert_fusion.2
  216.5 2.5 fusion.47
  219.8 4.2 %convolution_convert_fusion.1 = bf16[3072,768]{1,0:T(8,128)(2,1)} fusion(bf16[1,1,192,768]{3,2,1,0:T(8,128)(2,1)S(1)} %copy-done.22, f32[192,3072]{1,0:T(8,128)S(1)} %copy-done.19), kind=kOutput, calls=%fused_computation.1 | convolution fusion | flops 913637376 | bytes 7372800 | tf_op jit(solution)/shard_map/tf,td->fd/dot_general | solution.py:576
  224.1 2.2 fusion.14
  226.3 1.7 copy-done.8
  228.0 1.7 copy-done.9
  229.7 10.5 %attention_key_gradients.1 = (f32[192,768]{1,0:T(8,128)S(1)}, f32[192,768]{1,0:T(8,128)S(1)}) custom-call(s32[192,1]{1,0:T(8,128)S(1)} %add_select_fusion.qpos_ref.kpos_ref, s32[1,1536]{1,0:T(1,128)S(1)} %select_n.40.kpos_ref.qpos_ref, bf16[192,1536]{1,0:T(8,128)(2,1)S(1)} %copy-done.7, bf16[192,1536]{1,0:T(8,128)(2,1)S(1)} %copy-done.7, ...), custom_call_target="tpu_custom_call" | custom-call | flops 3623878656 | bytes 4718592 | tf_op jit(solution)/shard_map/attention_key_gradients/pallas_call | solution.py:219
  240.4 2.7 fusion.32
  243.1 1.2 convolution_convert_fusion
  244.8 1.1 constant_dynamic-update-slice_fusion.9
  246.7 1.1 constant_dynamic-update-slice_fusion.8
  247.8 1.2 constant_dynamic-update-slice_fusion.7
  249.0 1.1 constant_dynamic-update-slice_fusion.6
  250.0 1.1 constant_dynamic-update-slice_fusion.5
  251.1 1.1 constant_dynamic-update-slice_fusion.4
  252.3 1.1 constant_dynamic-update-slice_fusion.3
  253.4 1.1 constant_dynamic-update-slice_fusion.2
  254.5 4.7 %constant_dynamic-update-slice_fusion.1 = bf16[4,2,4,304,768]{4,3,2,1,0:T(8,128)(2,1)} fusion(bf16[4,2,4,304,768]{4,3,2,1,0:T(8,128)(2,1)} %constant_dynamic-update-slice_fusion.2, bf16[4,2,4,96,768]{4,3,2,1,0:T(8,128)(2,1)} %bitcast.104), kind=kLoop, calls=%fused_computation.70 | loop fusion | bytes 9437184
  259.2 0.9 constant_dynamic-update-slice_fusion.packed
  260.2 106.3 %sum_gradients.1 = f32[304,768]{1,0:T(8,128)S(1)} custom-call(bf16[4,2,4,304,768]{4,3,2,1,0:T(8,128)(2,1)} %constant_dynamic-update-slice_fusion.packed), custom_call_target="tpu_custom_call" | custom-call | tf_op jit(solution)/shard_map/sum_gradients/pallas_call | solution.py:469
  367.8 1.4 reshape.322
  369.2 1.6 fusion.50
  370.8 1.3 slice.159
  372.1 0.7 slice.139
  372.8 2.1 fusion.31
  (166 shorter events, 12.1 us)
Async XLA Ops:
  7.2 3.1 copy-start
  7.2 153.0 %all-gather.5.cloned.1.call-start = ((), (), s32[]{:S(2)}) async-start(), calls=%async_computation | async-start | bytes 5308416 | tf_op jit(solution)/shard_map/all_gather | solution.py:539
  12.0 101.8 %copy-start.29 = (f32[192]{0:T(256)}, f32[192]{0:T(256)S(1)}, u32[]{:S(2)}) copy-start(f32[192]{0:T(256)S(1)} %broadcast_multiply_fusion.5) | copy-start | bytes 2308
  13.3 100.6 %copy-start.38 = (f32[192]{0:T(256)}, f32[192]{0:T(256)S(1)}, u32[]{:S(2)}) copy-start(f32[192]{0:T(256)S(1)} %add_rsqrt_fusion.1) | copy-start | bytes 2308
  110.3 3.5 copy-start.16
  110.4 3.5 copy-start.35
  110.4 3.5 copy-start.48
  110.4 3.5 copy-start.50
  113.7 2.7 copy-start.52
  113.8 112.6 %all-gather.7.cloned.1.call-start = ((), (), s32[]{:S(2)}) async-start(), calls=%async_computation.1 | async-start | bytes 2654208 | tf_op jit(solution)/shard_map/all_gather | solution.py:543
  116.4 110.0 %all-gather.9.cloned.1.call-start = ((), (), s32[]{:S(2)}) async-start(), calls=%async_computation.2 | async-start | bytes 2654208 | tf_op jit(solution)/shard_map/all_gather | solution.py:572
  160.2 2.3 copy-start.2
  163.5 10.7 %copy-start.15 = (bf16[4,8,24,768]{3,2,1,0:T(8,128)(2,1)S(1)}, bf16[4,8,24,768]{3,2,1,0:T(8,128)(2,1)}, u32[]{:S(2)}) copy-start(bf16[4,8,24,768]{3,2,1,0:T(8,128)(2,1)} %get-tuple-element.25) | copy-start | bytes 3538948
  163.5 10.7 %copy-start.34 = (f32[768]{0:T(1024)S(1)}, f32[768]{0:T(1024)}, u32[]{:S(2)}) copy-start(f32[768]{0:T(1024)} %param.21) | copy-start | bytes 9220
  163.5 11.4 %copy-start.10 = (bf16[4,8,24,3072]{3,2,1,0:T(8,128)(2,1)S(1)}, bf16[4,8,24,3072]{3,2,1,0:T(8,128)(2,1)}, u32[]{:S(2)}) copy-start(bf16[4,8,24,3072]{3,2,1,0:T(8,128)(2,1)} %get-tuple-element.26) | copy-start | bytes 14155780
  174.7 2.2 slice-start
  174.9 2.2 slice-start.1
  176.1 4.1 %copy-start.18 = (f32[192,3072]{1,0:T(8,128)}, f32[192,3072]{1,0:T(8,128)S(1)}, u32[]{:S(2)}) copy-start(f32[192,3072]{1,0:T(8,128)S(1)} %convolution_add_fusion) | copy-start | bytes 7077892
  180.2 2.4 copy-start.20
  185.1 13.8 %copy-start.5 = (bf16[192,768]{1,0:T(8,128)(2,1)S(1)}, bf16[192,768]{1,0:T(8,128)(2,1)}, u32[]{:S(2)}) copy-start(bf16[192,768]{1,0:T(8,128)(2,1)} %fusion.15.q_ref) | copy-start | bytes 884740
  185.2 13.8 %copy-start.6 = (bf16[192,768]{1,0:T(8,128)(2,1)S(1)}, bf16[192,768]{1,0:T(8,128)(2,1)}, u32[]{:S(2)}) copy-start(bf16[192,768]{1,0:T(8,128)(2,1)} %get-tuple-element.74.do_ref) | copy-start | bytes 884740
  199.0 2.4 copy-start.3
  201.4 8.5 %copy-start.32 = (bf16[768]{0:T(1024)(128)(2,1)S(1)}, bf16[768]{0:T(1024)(128)(2,1)}, u32[]{:S(2)}) copy-start(bf16[768]{0:T(1024)(128)(2,1)} %get-tuple-element.39) | copy-start | bytes 4612
  201.4 8.6 %copy-start.33 = (bf16[3072]{0:T(1024)(128)(2,1)S(1)}, bf16[3072]{0:T(1024)(128)(2,1)}, u32[]{:S(2)}) copy-start(bf16[3072]{0:T(1024)(128)(2,1)} %get-tuple-element.76) | copy-start | bytes 18436
  201.4 9.3 %copy-start.42 = (bf16[768]{0:T(1024)(128)(2,1)S(1)}, bf16[768]{0:T(1024)(128)(2,1)}, u32[]{:S(2)}) copy-start(bf16[768]{0:T(1024)(128)(2,1)} %get-tuple-element.31) | copy-start | bytes 4612
  201.4 10.0 %copy-start.41 = (bf16[768]{0:T(1024)(128)(2,1)S(1)}, bf16[768]{0:T(1024)(128)(2,1)}, u32[]{:S(2)}) copy-start(bf16[768]{0:T(1024)(128)(2,1)} %get-tuple-element.37) | copy-start | bytes 4612
  216.5 3.1 copy-start.19
  216.5 3.3 copy-start.22
  216.5 7.5 %slice-start.2 = ((s8[4718592]{0:T(1024)(128)(4,1)}), s8[4194304]{0:T(1024)(128)(4,1)S(1)}, s32[]{:S(2)}) async-start(s8[4718592]{0:T(1024)(128)(4,1)} %bitcast.115), calls=%async_computation.5 | async-start | bytes 8388608
  219.8 4.2 %slice-start.3 = ((s8[4718592]{0:T(1024)(128)(4,1)}), s8[524288]{0:T(1024)(128)(4,1)S(1)}, s32[]{:S(2)}) async-start(s8[4718592]{0:T(1024)(128)(4,1)} %bitcast.115), calls=%async_computation.6 | async-start | bytes 1048576
  219.8 4.2 %copy-start.49 = (f32[768]{0:T(1024)S(1)}, f32[768]{0:T(1024)}, u32[]{:S(2)}) copy-start(f32[768]{0:T(1024)} %param.25) | copy-start | bytes 9220
  224.1 2.3 copy-start.7
  224.1 16.2 %copy-start.30 = (f32[192]{0:T(256)S(1)}, f32[192]{0:T(256)}, u32[]{:S(2)}) copy-start(f32[192]{0:T(256)} %copy-done.29) | copy-start | bytes 2308
  224.1 16.2 %copy-start.36 = (f32[768]{0:T(1024)S(1)}, f32[768]{0:T(1024)}, u32[]{:S(2)}) copy-start(f32[768]{0:T(1024)} %param.26) | copy-start | bytes 9220
  224.1 16.2 %copy-start.39 = (f32[192]{0:T(256)S(1)}, f32[192]{0:T(256)}, u32[]{:S(2)}) copy-start(f32[192]{0:T(256)} %copy-done.38) | copy-start | bytes 2308
  229.7 10.7 %copy-start.47 = (bf16[4,8,24,2304]{3,2,1,0:T(8,128)(2,1)S(1)}, bf16[4,8,24,2304]{3,2,1,0:T(8,128)(2,1)}, u32[]{:S(2)}) copy-start(bf16[4,8,24,2304]{3,2,1,0:T(8,128)(2,1)} %get-tuple-element.23) | copy-start | bytes 10616836
  240.3 2.7 copy-start.51
  246.6 2.3 copy-start.17
  247.8 2.2 copy-start.14
  248.9 2.2 copy-start.13
  250.0 2.2 copy-start.12
  251.1 2.2 copy-start.11
  260.2 112.6 %copy-start.46 = (f32[192]{0:T(256)S(1)}, f32[192]{0:T(256)}, u32[]{:S(2)}) copy-start(f32[192]{0:T(256)} %get-tuple-element.34) | copy-start | bytes 2308
  260.2 112.6 %copy-start.45 = (f32[192]{0:T(256)S(1)}, f32[192]{0:T(256)}, u32[]{:S(2)}) copy-start(f32[192]{0:T(256)} %get-tuple-element.35) | copy-start | bytes 2308
  260.2 112.6 %copy-start.31 = (f32[192]{0:T(256)S(1)}, f32[192]{0:T(256)}, u32[]{:S(2)}) copy-start(f32[192]{0:T(256)} %copy-done.29) | copy-start | bytes 2308
  260.2 112.6 %copy-start.37 = (f32[768]{0:T(1024)S(1)}, f32[768]{0:T(1024)}, u32[]{:S(2)}) copy-start(f32[768]{0:T(1024)} %param.26) | copy-start | bytes 9220
  260.2 112.7 %copy-start.40 = (f32[192]{0:T(256)S(1)}, f32[192]{0:T(256)}, u32[]{:S(2)}) copy-start(f32[192]{0:T(256)} %copy-done.38) | copy-start | bytes 2308
  260.2 116.2 %copy-start.1 = (bf16[192,3072]{1,0:T(8,128)(2,1)S(1)}, bf16[192,3072]{1,0:T(8,128)(2,1)}, u32[]{:S(2)}) copy-start(bf16[192,3072]{1,0:T(8,128)(2,1)} %param.22) | copy-start | bytes 3538948
  (12 other events, 16.2 us)
Sparse Core Ops, SparseCore 0:
  113.9 46.2 all-gather.4
  162.6 29.0 all-gather.6
  194.2 29.0 all-gather.8
